TPU v7x, 256 devices: a whole 4x4x8 slice. The times are simulated.
256 devices in a mesh: dp: 64 (over z, x, core), tp: 4 (over y).
Axes of the slice: x: 4, y: 4, z: 8, core: 2. Of those that a mesh axis runs over, the one named last changes fastest.
Arguments:
- hidden: bfloat16 [2048, 4096], P('dp', 'tp'), may hold values from -6 to 6
- routes: int32 [2048, 8], P('dp'), may hold values from 0 to 63, all different within a row; in each aligned block of 32 rows (0 to 31, 32 to 63, ...) at most 8 rows name the same one
- routing_weights: float32 [2048, 8], P('dp'), may hold values from 0.05 to 1
- w_gate: bfloat16 [64, 4096, 1536], P('dp', None, 'tp'), may hold values from -0.09375 to 0.09375
- w_up: bfloat16 [64, 4096, 1536], P('dp', None, 'tp'), may hold values from -0.09375 to 0.09375
- w_down: bfloat16 [64, 1536, 4096], P('dp', 'tp'), may hold values from -0.15625 to 0.15625
- norm_gain: float32 [4096], replicated, may hold values from 0.1 to 1.9
- key_projection_weight: bfloat16 [4096, 512], P(None, 'tp'), may hold values from -0.09375 to 0.09375
- value_projection_weight: bfloat16 [4096, 512], P(None, 'tp'), may hold values from -0.09375 to 0.09375
- queries: bfloat16 [2048, 8192], P('dp', 'tp'), may hold values from -128 to 128
- cached_key_rows: bfloat16 [64, 128, 512], P('dp', None, 'tp'), may hold values from -4 to 4
- cached_value_rows: bfloat16 [64, 128, 512], P('dp', None, 'tp'), may hold values from -6 to 6
- lengths: int32 [64], P('dp'), may hold values from 16 to 128
- parents: int32 [64, 32], P('dp'), may hold values from -1 to 30, as said below
Outputs:
- layer_output: bfloat16 [2048, 4096], P('dp', 'tp')
- next_layer_keys: bfloat16 [2048, 512], P('dp', 'tp')
- next_layer_values: bfloat16 [2048, 512], P('dp', 'tp')
- attended: bfloat16 [2048, 8192], P('dp', 'tp')
Inputs may be any that keep to these rules, and one draw needn't show every extreme that they name: `routes`: each row names 8 different experts. In each aligned block of 32 rows (the rows of one device) no expert is named by more than 8 rows, a bound that some block reaches. `parents`: node 0 of each request is the root, with parent -1; every other node i has its parent among nodes max(0, i - 8) to i - 1.
All inputs are finite; a program needn't handle non-finite values.
Results may differ from a plain program's by a relative error of at most 0.013.
Values may be sent and summed in bfloat16 or wider, within the bound.
No kernel may reach another device: no remote copies, remote signals or barrier semaphores. Data moves between devices by JAX's collectives and lax.ppermute only.
A program may use at most 64 MiB of HBM per device.

v0:
```python
import math
import jax
import jax.numpy as jnp
from jax import lax
from jax.sharding import PartitionSpec as P

HEAD_SIZE = 128


def split_up(shard, dim, size):
    shape = shard.shape
    tiles = shard.reshape(*shape[:dim], size, shape[dim] // size, *shape[dim + 1 :])
    return jnp.moveaxis(tiles, dim, 0)


def sent_and_summed(shard, axis, dim):
    size = lax.axis_size(axis)
    tiles = lax.all_to_all(split_up(shard, dim, size), axis, 0, 0, tiled=True)
    return jnp.sum(tiles.astype(jnp.float32), axis=0)


def joined_along(tiles, dim):
    shape = list(tiles.shape[1:])
    shape[dim] *= tiles.shape[0]
    return jnp.moveaxis(tiles, 0, dim).reshape(shape)


def copy_for_each(shard, axis):
    copies = jnp.broadcast_to(shard, (lax.axis_size(axis), *shard.shape))
    return lax.all_to_all(copies, axis, split_axis=0, concat_axis=0, tiled=True)


def gathered_copies(shard, axis, dim):
    return joined_along(copy_for_each(shard, axis), dim)


def ancestry(parent_row):
    node_count = parent_row.shape[0]
    position = jnp.arange(node_count, dtype=jnp.int32)
    reached = (parent_row[:, None] == position[None, :]).astype(jnp.float32)
    reached = reached + jnp.eye(node_count, dtype=jnp.float32)
    for doubling in range((node_count - 1).bit_length()):
        reached = jnp.minimum(jnp.dot(reached, reached, preferred_element_type=jnp.float32), 1.0)
    return reached > 0.5


def quarter_to_whole(received):
    return lax.all_gather(received, "tp", axis=2, tiled=True)


def attend_local(
    queries, cached_key_rows, cached_value_rows, tree_key_rows, tree_value_rows, lengths, parents
):
    request_count = lengths.shape[0]
    node_count = parents.shape[1]
    slot_length = cached_key_rows.shape[1]
    kv_local = cached_key_rows.shape[2] // HEAD_SIZE
    query_group_count = queries.shape[1] // (kv_local * HEAD_SIZE)
    scaled = 1.0 / math.sqrt(HEAD_SIZE)
    tree_query_block = queries.reshape(
        request_count, node_count, kv_local, query_group_count, HEAD_SIZE
    )
    joined_key_block = cached_key_rows.reshape(request_count, slot_length, kv_local, HEAD_SIZE)
    joined_value_block = cached_value_rows.reshape(request_count, slot_length, kv_local, HEAD_SIZE)
    tree_key_block = tree_key_rows.reshape(request_count, node_count, kv_local, HEAD_SIZE)
    tree_value_block = tree_value_rows.reshape(request_count, node_count, kv_local, HEAD_SIZE)
    cache_scores = (
        jnp.einsum(
            "rnkgd,rpkd->rkgnp",
            tree_query_block,
            joined_key_block,
            preferred_element_type=jnp.float32,
        )
        * scaled
    )
    tree_scores = (
        jnp.einsum(
            "rnkgd,rmkd->rkgnm",
            tree_query_block,
            tree_key_block,
            preferred_element_type=jnp.float32,
        )
        * scaled
    )
    visible = jnp.arange(slot_length, dtype=jnp.int32)[None, :] < lengths[:, None]
    cache_scores = jnp.where(visible[:, None, None, None, :], cache_scores, -1e30)
    related = jax.vmap(ancestry)(parents)
    tree_scores = jnp.where(related[:, None, None], tree_scores, -1e30)
    highest = jnp.maximum(jnp.max(cache_scores, axis=-1), jnp.max(tree_scores, axis=-1))[..., None]
    cache_raised = jnp.exp(cache_scores - highest)
    tree_raised = jnp.exp(tree_scores - highest)
    denominator = jnp.sum(cache_raised, axis=-1, keepdims=True) + jnp.sum(
        tree_raised, axis=-1, keepdims=True
    )
    cache_weights = (cache_raised / denominator).astype(jnp.bfloat16)
    tree_weights = (tree_raised / denominator).astype(jnp.bfloat16)
    output = jnp.einsum(
        "rkgnp,rpkd->rnkgd", cache_weights, joined_value_block, preferred_element_type=jnp.float32
    )
    output = output + jnp.einsum(
        "rkgnm,rmkd->rnkgd", tree_weights, tree_value_block, preferred_element_type=jnp.float32
    )
    return output.reshape(request_count * node_count, -1).astype(jnp.bfloat16)


def on_device(
    hidden,
    routes,
    routing_weights,
    w_gate,
    w_up,
    w_down,
    norm_gain,
    key_projection_weight,
    value_projection_weight,
    queries,
    cached_key_rows,
    cached_value_rows,
    lengths,
    parents,
):
    token_count = hidden.shape[0]
    top_count = routes.shape[1]
    local_experts = w_gate.shape[0]
    expert_count = lax.axis_size("dp") * local_experts
    capacity = min(token_count, 2 * token_count * top_count // expert_count)
    column_count = hidden.shape[1]
    weights = routing_weights / jnp.sum(routing_weights, axis=1, keepdims=True)
    expert_ids = jnp.arange(expert_count, dtype=jnp.int32)
    chosen = routes[:, :, None] == expert_ids[None, None, :]
    member = jnp.any(chosen, axis=1)
    portion = jnp.sum(jnp.where(chosen, weights[:, :, None], 0.0), axis=1)
    earlier = jnp.tril(jnp.ones((token_count, token_count), jnp.bfloat16), -1)
    rank = jnp.dot(earlier, member.astype(jnp.bfloat16), preferred_element_type=jnp.float32)
    slots = jnp.arange(capacity, dtype=jnp.float32)
    placed = member.T[:, None, :] & (rank.T[:, None, :] == slots[None, :, None])
    placed = placed.reshape(expert_count * capacity, token_count)
    outgoing = jnp.dot(
        placed.astype(jnp.bfloat16), hidden, preferred_element_type=jnp.float32
    ).astype(jnp.bfloat16)
    outgoing = outgoing.reshape(expert_count, capacity, column_count)
    received = quarter_to_whole(
        lax.all_to_all(outgoing, "dp", split_axis=0, concat_axis=0, tiled=True)
    )
    slot_count = received.shape[1]
    grouped = received.reshape(-1, local_experts, slot_count, received.shape[2])
    gate_act = jnp.einsum("secd,edf->secf", grouped, w_gate, preferred_element_type=jnp.float32)
    upward = jnp.einsum("secd,edf->secf", grouped, w_up, preferred_element_type=jnp.float32)
    active = (jax.nn.silu(gate_act) * upward).astype(jnp.bfloat16)
    partial_value = jnp.einsum("secf,efd->secd", active, w_down, preferred_element_type=jnp.float32)
    partial_value = partial_value.reshape(received.shape[0], slot_count, partial_value.shape[3])
    summed = sent_and_summed(partial_value.astype(jnp.bfloat16), "tp", 2)
    back = lax.all_to_all(
        summed.astype(jnp.bfloat16), "dp", split_axis=0, concat_axis=0, tiled=True
    )
    flat_back = back.reshape(expert_count * capacity, back.shape[2])
    spread = jnp.broadcast_to(portion.T[:, None, :], (expert_count, capacity, token_count))
    spread = jnp.where(placed, spread.reshape(expert_count * capacity, token_count), 0.0)
    upper = spread.astype(jnp.bfloat16)
    lower = (spread - upper.astype(jnp.float32)).astype(jnp.bfloat16)
    both = jnp.concatenate([upper, lower], axis=1)
    mixed = lax.dot_general(
        both, flat_back, (((0,), (0,)), ((), ())), preferred_element_type=jnp.float32
    )
    expert_mix = mixed[:token_count] + mixed[token_count:]
    own_out = (hidden.astype(jnp.float32) + expert_mix).astype(jnp.bfloat16)
    full_out = gathered_copies(own_out, "tp", 1)
    widened = full_out.astype(jnp.float32)
    scaling = lax.rsqrt(jnp.mean(widened * widened, axis=1, keepdims=True) + 1e-06)
    normed = (widened * scaling * norm_gain).astype(jnp.bfloat16)
    tree_key_rows = jnp.dot(
        normed, key_projection_weight, preferred_element_type=jnp.float32
    ).astype(jnp.bfloat16)
    tree_value_rows = jnp.dot(
        normed, value_projection_weight, preferred_element_type=jnp.float32
    ).astype(jnp.bfloat16)
    attended = attend_local(
        queries,
        cached_key_rows,
        cached_value_rows,
        tree_key_rows,
        tree_value_rows,
        lengths,
        parents,
    )
    return (own_out, tree_key_rows, tree_value_rows, attended)


def solution(mesh):
    return jax.shard_map(
        on_device,
        mesh=mesh,
        in_specs=(
            P("dp", "tp"),
            P("dp", None),
            P("dp", None),
            P("dp", None, "tp"),
            P("dp", None, "tp"),
            P("dp", "tp", None),
            P(),
            P(None, "tp"),
            P(None, "tp"),
            P("dp", "tp"),
            P("dp", None, "tp"),
            P("dp", None, "tp"),
            P("dp"),
            P("dp", None),
        ),
        out_specs=(P("dp", "tp"), P("dp", "tp"), P("dp", "tp"), P("dp", "tp")),
        check_vma=False,
    )
```

profile of v0, /device:TPU:2, one launch (start us, length us, event | category | flops | bytes accessed | tf_op | source)
XLA Modules:
  0.0 239.4 jit_solution(4586139410621288270)
XLA Ops:
  7.2 0.9 copy.67
  8.2 0.7 reduce_sum.57
  8.9 0.7 broadcast_divide_fusion
  10.9 1.3 fusion.5
  12.2 40.7 %all_to_all.20 = bf16[64,8,1024]{2,1,0:T(8,128)(2,1)} all-to-all(bf16[64,8,1024]{2,1,0:T(8,128)(2,1)S(1)} %fusion.5), channel_id=1, replica_groups=mesh['dp'=64,'tp'=4] {'dp'}, dimensions={0} | all-to-all | bytes 2097152 | tf_op jit(solution)/shard_map/all_to_all | solution.py:143
  52.9 47.6 %all-gather.2.cloned.1.call-done = bf16[64,8,4096]{2,1,0:T(8,128)(2,1)} async-done(((bf16[64,8,1024]{2,1,0:T(8,128)(2,1)}), bf16[64,8,4096]{2,1,0:T(8,128)(2,1)}) %all-gather.2.cloned.1.call-update) | async-done | bytes 4194320 | tf_op jit(solution)/shard_map/all_gather | solution.py:48
  100.5 6.4 %fusion.6 = f32[64,1,8,384]{3,2,0,1:T(8,128)} fusion(bf16[64,8,4096]{2,1,0:T(8,128)(2,1)} %all-gather.2.cloned.1.call-done, bf16[1,4096,384]{2,1,0:T(8,128)(2,1)} %param.17), kind=kOutput, calls=%fused_computation.9 | convolution fusion | flops 1610612736 | bytes 8126464 | tf_op jit(solution)/shard_map/secd,edf->secf/dot_general | solution.py:147
  107.0 9.7 %convolution_convert_fusion = bf16[64,8,4096]{2,1,0:T(8,128)(2,1)} fusion(bf16[1,384,4096]{2,1,0:T(8,128)(2,1)S(1)} %copy-done, bf16[64,8,4096]{2,1,0:T(8,128)(2,1)} %all-gather.2.cloned.1.call-done, bf16[1,4096,384]{2,1,0:T(8,128)(2,1)} %param.18, f32[64,1,8,384]{3,2,0,1:T(8,128)} %fusion.6), kind=kOutput, calls=%fused_computation | convolution fusion | flops 3224502272 | bytes 15466496 | tf_op jit(solution)/shard_map/secf,efd->secd/dot_general | solution.py:150
  116.7 2.6 %copy.101 = bf16[64,8,4,1024]{3,1,0,2:T(8,128)(2,1)S(1)} copy(bf16[64,8,4,1024]{3,1,2,0:T(8,128)(2,1)} %bitcast.160) | data formatting | bytes 8388608 | tf_op jit(solution)/shard_map/convert_element_type | solution.py:152
  119.3 52.5 %all_to_all.21 = bf16[4,64,8,1024]{3,2,1,0:T(8,128)(2,1)} all-to-all(bf16[4,64,8,1024]{3,2,1,0:T(8,128)(2,1)S(1)} %bitcast.157), channel_id=1, replica_groups=mesh['dp'=64,'tp'=4] {'tp'}, dimensions={0} | all-to-all | bytes 8388608 | tf_op jit(solution)/shard_map/all_to_all | solution.py:18
  171.8 4.4 %reduce_sum.59 = bf16[64,8,1024]{2,1,0:T(8,128)(2,1)} reduce(bf16[4,64,8,1024]{3,2,1,0:T(8,128)(2,1)} %all_to_all.21, bf16[]{:T(256)} %constant.15.clone.1), dimensions={0}, to_apply=%region_3.4 | reduce | flops 1572864 | bytes 5242882 | tf_op jit(solution)/shard_map/reduce_sum | solution.py:19
  176.2 10.8 %all-to-all-start.2 = ((bf16[64,8,1024]{2,1,0:T(8,128)(2,1)}), bf16[64,8,1024]{2,1,0:T(8,128)(2,1)}, u32[]{:S(2)}, u32[]{:S(2)}) async-start(bf16[64,8,1024]{2,1,0:T(8,128)(2,1)} %reduce_sum.59), calls=%async_computation.2 | async-start | bytes 2097152 | tf_op jit(solution)/shard_map/all_to_all | solution.py:153
  187.8 0.7 copy.78
  189.1 0.5 iota_compare_fusion.2
  189.7 26.1 %all-to-all-done.2 = bf16[64,8,1024]{2,1,0:T(8,128)(2,1)} async-done(((bf16[64,8,1024]{2,1,0:T(8,128)(2,1)}), bf16[64,8,1024]{2,1,0:T(8,128)(2,1)}, u32[]{:S(2)}, u32[]{:S(2)}) %all-to-all-start.2) | async-done | bytes 1048608 | tf_op jit(solution)/shard_map/all_to_all | solution.py:153
  215.8 1.6 fusion.29
  217.4 0.7 broadcast_in_dim.81
  218.1 3.4 %all-to-all-start.3 = ((bf16[4,32,1024]{2,1,0:T(8,128)(2,1)}), bf16[4,32,1024]{2,1,0:T(8,128)(2,1)S(1)}, u32[]{:S(2)}, u32[]{:S(2)}) async-start(bf16[4,32,1024]{2,1,0:T(8,128)(2,1)} %broadcast_in_dim.81), calls=%async_computation.3 | async-start | bytes 524288 | tf_op jit(solution)/shard_map/all_to_all | solution.py:30
  221.5 2.4 %fusion.71 = (f32[16,32]{1,0:T(8,128)}, f32[1,1,16,32,128]{4,3,2,1,0:T(8,128)}) fusion(bf16[1,128,128]{2,1,0:T(8,128)(2,1)} %param.24, pred[128]{0:T(512)(128)(4,1)} %iota_compare_fusion.2, bf16[32,2048]{1,0:T(8,128)(2,1)} %param.23), kind=kOutput, calls=%fused_computation.96 | convolution fusion | flops 16973312 | bytes 428160 | tf_op jit(solution)/shard_map/rnkgd,rpkd->rkgnp/dot_general | solution.py:68
  223.9 4.2 %all-to-all-done.3 = bf16[4,32,1024]{2,1,0:T(8,128)(2,1)S(1)} async-done(((bf16[4,32,1024]{2,1,0:T(8,128)(2,1)}), bf16[4,32,1024]{2,1,0:T(8,128)(2,1)S(1)}, u32[]{:S(2)}, u32[]{:S(2)}) %all-to-all-start.3) | async-done | bytes 262176 | tf_op jit(solution)/shard_map/all_to_all | solution.py:30
  228.5 1.7 convolution_convert_fusion.3
  230.9 0.3 convolution_convert_fusion.2
  231.3 0.3 convolution_bitcast_fusion
  231.9 0.7 copy.102
  (61 shorter events, 3.4 us)
Async XLA Ops:
  7.2 99.8 %copy-start = (bf16[1,384,4096]{2,1,0:T(8,128)(2,1)S(1)}, bf16[1,384,4096]{2,1,0:T(8,128)(2,1)}, u32[]{:S(2)}) copy-start(bf16[1,384,4096]{2,1,0:T(8,128)(2,1)} %param.19) | copy-start | bytes 9437188
  7.2 93.3 %all-gather.2.cloned.1.call-start = ((), (), s32[]{:S(2)}) async-start(), calls=%async_computation.4 | async-start | bytes 5242880 | tf_op jit(solution)/shard_map/all_gather | solution.py:48
  171.8 15.3 %copy-start.11 = (s32[1,32]{1,0:T(1,128)S(1)}, s32[1,32]{1,0:T(1,128)}, u32[]{:S(2)}) copy-start(s32[1,32]{1,0:T(1,128)} %param.27) | copy-start | bytes 388
  176.2 41.1 %copy-start.4 = (bf16[32,1024]{1,0:T(8,128)(2,1)S(1)}, bf16[32,1024]{1,0:T(8,128)(2,1)}, u32[]{:S(2)}) copy-start(bf16[32,1024]{1,0:T(8,128)(2,1)} %param.14) | copy-start | bytes 196612
  176.2 39.6 %all-to-all-start.2 = ((bf16[64,8,1024]{2,1,0:T(8,128)(2,1)}), bf16[64,8,1024]{2,1,0:T(8,128)(2,1)}, u32[]{:S(2)}, u32[]{:S(2)}) async-start(bf16[64,8,1024]{2,1,0:T(8,128)(2,1)} %reduce_sum.59), calls=%async_computation.2 | async-start | bytes 2097152 | tf_op jit(solution)/shard_map/all_to_all | solution.py:153
  187.0 41.4 %copy-start.6 = (f32[4096]{0:T(1024)S(1)}, f32[4096]{0:T(1024)}, u32[]{:S(2)}) copy-start(f32[4096]{0:T(1024)} %param.20) | copy-start | bytes 49156
  215.8 14.4 %copy-start.3 = (bf16[32,2048]{1,0:T(8,128)(2,1)S(1)}, bf16[32,2048]{1,0:T(8,128)(2,1)}, u32[]{:S(2)}) copy-start(bf16[32,2048]{1,0:T(8,128)(2,1)} %param.23) | copy-start | bytes 393220
  217.4 0.7 copy-start.5
  218.1 10.1 %all-to-all-start.3 = ((bf16[4,32,1024]{2,1,0:T(8,128)(2,1)}), bf16[4,32,1024]{2,1,0:T(8,128)(2,1)S(1)}, u32[]{:S(2)}, u32[]{:S(2)}) async-start(bf16[4,32,1024]{2,1,0:T(8,128)(2,1)} %broadcast_in_dim.81), calls=%async_computation.3 | async-start | bytes 524288 | tf_op jit(solution)/shard_map/all_to_all | solution.py:30
  228.2 2.0 copy-start.9
  228.2 2.4 copy-start.8
  228.2 2.5 %copy-start.2 = (f32[1,1,16,32,128]{4,3,2,1,0:T(8,128)S(1)}, f32[1,1,16,32,128]{4,3,2,1,0:T(8,128)}, u32[]{:S(2)}) copy-start(f32[1,1,16,32,128]{4,3,2,1,0:T(8,128)} %get-tuple-element.7) | copy-start | bytes 786436
  228.2 2.7 %copy-start.1 = (bf16[4096,128]{1,0:T(8,128)(2,1)S(1)}, bf16[4096,128]{1,0:T(8,128)(2,1)}, u32[]{:S(2)}) copy-start(bf16[4096,128]{1,0:T(8,128)(2,1)} %param.22) | copy-start | bytes 3145732
  228.2 3.1 %copy-start.12 = (bf16[1,128,128]{2,1,0:T(8,128)(2,1)S(1)}, bf16[1,128,128]{2,1,0:T(8,128)(2,1)}, u32[]{:S(2)}) copy-start(bf16[1,128,128]{2,1,0:T(8,128)(2,1)} %param.25) | copy-start | bytes 98308
  230.2 2.4 %copy-start.7 = (bf16[32,128]{1,0:T(8,128)(2,1)}, bf16[32,128]{1,0:T(8,128)(2,1)S(1)}, u32[]{:S(2)}) copy-start(bf16[32,128]{1,0:T(8,128)(2,1)S(1)} %convolution_convert_fusion.3) | copy-start | bytes 24580
  231.2 1.4 copy-start.10
Sparse Core Ops, SparseCore 0:
  53.0 47.4 all-gather.1
where the time goes:
time: 240 us; the launch traced here: 239 us
  blocking collectives  93.2 us (39%)
  waiting for transfers between devices  77.9 us (32%)
  matrix products  25.2 us (10%)
  between operations  15 us (6%)
  starting transfers between devices  14.3 us (6%)
  other arithmetic  7.3 us (3%)
  local copies, waits for them, and re-layouts  6.57 us (3%)
    all_to_all x1, blocking collectives, sent_and_summed(): tiles = lax.all_to_all(split_up(shard, dim, size), axis, 0, 0, tiled=True)  52.5 us
    all_gather x1, waiting for transfers between devices, quarter_to_whole(): return lax.all_gather(received, 'tp', axis=2, tiled=True)  47.6 us
    all_to_all x1, blocking collectives, on_device(): lax.all_to_all(outgoing, 'dp', split_axis=0, concat_axis=0, tiled=True)  40.7 us
    all_to_all x1, waiting for transfers between devices, on_device(): lax.all_to_all(summed.astype(jnp.bfloat16), 'dp', split_axis=0, concat_ax...  26.1 us
    all_to_all x1, starting transfers between devices, on_device(): lax.all_to_all(summed.astype(jnp.bfloat16), 'dp', split_axis=0, concat_ax...  10.8 us
    dot_general x1, matrix products, on_device(): jnp.einsum('secf,efd->secd', active, w_down, preferred_element_type=jnp.f...  9.74 us
    dot_general x1, matrix products, on_device(): jnp.einsum('secd,edf->secf', grouped, w_gate, preferred_element_type=jnp....  6.43 us
  transfers between devices with their start and end apart: 3, of which 3 were waited for; matrix products, arithmetic and copies ran while one was open for 2% of the time, Pallas kernels for 0%

commit v1 on v0

--- a/solution.py
+++ b/solution.py
@@ -45,7 +45,9 @@
 
 
 def quarter_to_whole(received):
-    return lax.all_gather(received, "tp", axis=2, tiled=True)
+    return jnp.concatenate(
+        lax.all_to_all(jnp.stack([received] * lax.axis_size("tp")), "tp", 0, 0), axis=2
+    )
 
 
 def attend_local(

time: 240 us -> 227 us (0.946)
  blocking collectives: 93.2 us -> 143 us
  waiting for transfers between devices: 77.9 us -> 32 us
  between operations: 15 us -> 1.62 us
  matrix products: 25.2 us -> 22.2 us
  local copies, waits for them, and re-layouts: 6.57 us -> 9.07 us
  starting transfers between devices: 14.3 us -> 11.8 us
    all_to_all x0 -> x1, blocking collectives: none -> 52.1 us  [quarter_to_whole(): lax.all_to_all(jnp.stack([received] * lax.axis_size('tp')), 'tp', 0, 0)]
    all_gather x1 -> x0, waiting for transfers between devices: 47.6 us -> none  [quarter_to_whole(): return lax.all_gather(received, 'tp', axis=2, tiled=True)]
    dot_general x1, matrix products: 6.43 us -> 3.26 us  [on_device(): jnp.einsum('secd,edf->secf', grouped, w_gate, preferred_element_type=jnp....]
    all_to_all x1, starting transfers between devices: 10.8 us -> 8.35 us  [on_device(): lax.all_to_all(summed.astype(jnp.bfloat16), 'dp', split_axis=0, concat_ax...]
    all_to_all x1, blocking collectives: 52.5 us -> 50 us  [sent_and_summed(): tiles = lax.all_to_all(split_up(shard, dim, size), axis, 0, 0, tiled=True)]
  transfers between devices with their start and end apart: 3 -> 2, of which waited for: 3 -> 2; matrix products, arithmetic and copies ran while one was open for 2% -> 1% of each run, Pallas kernels for 0% -> 0%
where the time goes in v1:
time: 227 us; the launch traced here: 226 us
  blocking collectives  143 us (63%)
  waiting for transfers between devices  32 us (14%)
  matrix products  22.2 us (10%)
  starting transfers between devices  11.8 us (5%)
  local copies, waits for them, and re-layouts  9.07 us (4%)
  other arithmetic  6.82 us (3%)
    all_to_all x1, blocking collectives, quarter_to_whole(): lax.all_to_all(jnp.stack([received] * lax.axis_size('tp')), 'tp', 0, 0)  52.1 us
    all_to_all x1, blocking collectives, sent_and_summed(): tiles = lax.all_to_all(split_up(shard, dim, size), axis, 0, 0, tiled=True)  50 us
    all_to_all x1, blocking collectives, on_device(): lax.all_to_all(outgoing, 'dp', split_axis=0, concat_axis=0, tiled=True)  40.6 us
    all_to_all x1, waiting for transfers between devices, on_device(): lax.all_to_all(summed.astype(jnp.bfloat16), 'dp', split_axis=0, concat_ax...  27.2 us
    dot_general x1, matrix products, on_device(): jnp.einsum('secf,efd->secd', active, w_down, preferred_element_type=jnp.f...  9.73 us
    all_to_all x1, starting transfers between devices, on_device(): lax.all_to_all(summed.astype(jnp.bfloat16), 'dp', split_axis=0, concat_ax...  8.35 us
    all_to_all x1, waiting for transfers between devices, copy_for_each(): return lax.all_to_all(copies, axis, split_axis=0, concat_axis=0, tiled=True)  4.84 us
  transfers between devices with their start and end apart: 2, of which 2 were waited for; matrix products, arithmetic and copies ran while one was open for 1% of the time, Pallas kernels for 0%

profile of v1, /device:TPU:2, one launch (start us, length us, event | category | flops | bytes accessed | tf_op | source)
XLA Modules:
  0.0 226.2 jit_solution(8867648091934484067)
XLA Ops:
  0.7 0.9 copy.70
  1.6 0.7 reduce_sum.57
  2.3 0.7 broadcast_divide_fusion
  4.3 1.3 fusion.5
  5.6 40.6 %all_to_all.25 = bf16[64,8,1024]{2,1,0:T(8,128)(2,1)S(1)} all-to-all(bf16[64,8,1024]{2,1,0:T(8,128)(2,1)S(1)} %fusion.5), channel_id=1, replica_groups=mesh['dp'=64,'tp'=4] {'dp'}, dimensions={0} | all-to-all | bytes 2097152 | tf_op jit(solution)/shard_map/all_to_all | solution.py:145
  46.2 0.5 stack.2
  46.8 52.1 %all_to_all.26 = bf16[4,64,8,1024]{3,2,1,0:T(8,128)(2,1)S(1)} all-to-all(bf16[4,64,8,1024]{3,2,1,0:T(8,128)(2,1)S(1)} %stack.2), channel_id=1, replica_groups=mesh['dp'=64,'tp'=4] {'tp'}, dimensions={0} | all-to-all | bytes 8388608 | tf_op jit(solution)/shard_map/all_to_all | solution.py:49
  98.8 0.6 copy.78
  99.5 1.9 copy-done.1
  101.4 3.3 %fusion.6 = f32[64,1,8,384]{3,2,0,1:T(8,128)} fusion(bf16[64,8,4096]{2,1,0:T(8,128)(2,1)S(1)} %bitcast.163, bf16[1,4096,384]{2,1,0:T(8,128)(2,1)S(1)} %copy-done.11), kind=kOutput, calls=%fused_computation.9 | convolution fusion | flops 1610612736 | bytes 8126464 | tf_op jit(solution)/shard_map/secd,edf->secf/dot_general | solution.py:149
  104.7 9.7 %convolution_convert_fusion = bf16[64,8,4096]{2,1,0:T(8,128)(2,1)} fusion(bf16[1,384,4096]{2,1,0:T(8,128)(2,1)S(1)} %copy-done, bf16[64,8,4096]{2,1,0:T(8,128)(2,1)} %bitcast.164, bf16[1,4096,384]{2,1,0:T(8,128)(2,1)} %param.18, f32[64,1,8,384]{3,2,0,1:T(8,128)} %fusion.6), kind=kOutput, calls=%fused_computation | convolution fusion | flops 3224502272 | bytes 15466496 | tf_op jit(solution)/shard_map/secf,efd->secd/dot_general | solution.py:152
  114.4 2.6 %copy.105 = bf16[64,8,4,1024]{3,1,0,2:T(8,128)(2,1)S(1)} copy(bf16[64,8,4,1024]{3,1,2,0:T(8,128)(2,1)} %bitcast.165) | data formatting | bytes 8388608 | tf_op jit(solution)/shard_map/convert_element_type | solution.py:154
  117.1 50.0 %all_to_all.27 = bf16[4,64,8,1024]{3,2,1,0:T(8,128)(2,1)} all-to-all(bf16[4,64,8,1024]{3,2,1,0:T(8,128)(2,1)S(1)} %bitcast.160), channel_id=1, replica_groups=mesh['dp'=64,'tp'=4] {'tp'}, dimensions={0} | all-to-all | bytes 8388608 | tf_op jit(solution)/shard_map/all_to_all | solution.py:18
  167.1 4.4 %reduce_sum.59 = bf16[64,8,1024]{2,1,0:T(8,128)(2,1)} reduce(bf16[4,64,8,1024]{3,2,1,0:T(8,128)(2,1)} %all_to_all.27, bf16[]{:T(256)} %constant.15.clone.1), dimensions={0}, to_apply=%region_3.4 | reduce | flops 1572864 | bytes 5242882 | tf_op jit(solution)/shard_map/reduce_sum | solution.py:19
  171.5 8.4 %all-to-all-start.3 = ((bf16[64,8,1024]{2,1,0:T(8,128)(2,1)}), bf16[64,8,1024]{2,1,0:T(8,128)(2,1)}, u32[]{:S(2)}, u32[]{:S(2)}) async-start(bf16[64,8,1024]{2,1,0:T(8,128)(2,1)} %reduce_sum.59), calls=%async_computation.3 | async-start | bytes 2097152 | tf_op jit(solution)/shard_map/all_to_all | solution.py:155
  181.4 27.2 %all-to-all-done.3 = bf16[64,8,1024]{2,1,0:T(8,128)(2,1)} async-done(((bf16[64,8,1024]{2,1,0:T(8,128)(2,1)}), bf16[64,8,1024]{2,1,0:T(8,128)(2,1)}, u32[]{:S(2)}, u32[]{:S(2)}) %all-to-all-start.3) | async-done | bytes 1048608 | tf_op jit(solution)/shard_map/all_to_all | solution.py:155
  208.6 1.5 fusion.29
  210.2 0.7 broadcast_in_dim.81
  210.9 3.4 %all-to-all-start.4 = ((bf16[4,32,1024]{2,1,0:T(8,128)(2,1)}), bf16[4,32,1024]{2,1,0:T(8,128)(2,1)S(1)}, u32[]{:S(2)}, u32[]{:S(2)}) async-start(bf16[4,32,1024]{2,1,0:T(8,128)(2,1)} %broadcast_in_dim.81), calls=%async_computation.4 | async-start | bytes 524288 | tf_op jit(solution)/shard_map/all_to_all | solution.py:30
  214.3 1.8 fusion.71
  216.1 4.8 %all-to-all-done.4 = bf16[4,32,1024]{2,1,0:T(8,128)(2,1)S(1)} async-done(((bf16[4,32,1024]{2,1,0:T(8,128)(2,1)}), bf16[4,32,1024]{2,1,0:T(8,128)(2,1)S(1)}, u32[]{:S(2)}, u32[]{:S(2)}) %all-to-all-start.4) | async-done | bytes 262176 | tf_op jit(solution)/shard_map/all_to_all | solution.py:30
  221.2 1.7 convolution_convert_fusion.3
  222.9 1.2 fusion.72
  225.5 0.7 copy.106
  (61 shorter events, 3.7 us)
Async XLA Ops:
  0.6 104.1 %copy-start = (bf16[1,384,4096]{2,1,0:T(8,128)(2,1)S(1)}, bf16[1,384,4096]{2,1,0:T(8,128)(2,1)}, u32[]{:S(2)}) copy-start(bf16[1,384,4096]{2,1,0:T(8,128)(2,1)} %param.19) | copy-start | bytes 9437188
  98.8 2.6 %copy-start.11 = (bf16[1,4096,384]{2,1,0:T(8,128)(2,1)S(1)}, bf16[1,4096,384]{2,1,0:T(8,128)(2,1)}, u32[]{:S(2)}) copy-start(bf16[1,4096,384]{2,1,0:T(8,128)(2,1)} %param.17) | copy-start | bytes 9437188
  99.5 1.9 copy-start.1
  167.1 12.8 %copy-start.10 = (s32[1,32]{1,0:T(1,128)S(1)}, s32[1,32]{1,0:T(1,128)}, u32[]{:S(2)}) copy-start(s32[1,32]{1,0:T(1,128)} %param.27) | copy-start | bytes 388
  167.1 43.0 %copy-start.4 = (bf16[32,1024]{1,0:T(8,128)(2,1)S(1)}, bf16[32,1024]{1,0:T(8,128)(2,1)}, u32[]{:S(2)}) copy-start(bf16[32,1024]{1,0:T(8,128)(2,1)} %param.14) | copy-start | bytes 196612
  167.1 47.2 %copy-start.8 = (bf16[1,128,128]{2,1,0:T(8,128)(2,1)S(1)}, bf16[1,128,128]{2,1,0:T(8,128)(2,1)}, u32[]{:S(2)}) copy-start(bf16[1,128,128]{2,1,0:T(8,128)(2,1)} %param.24) | copy-start | bytes 98308
  171.5 49.7 %copy-start.6 = (f32[4096]{0:T(1024)S(1)}, f32[4096]{0:T(1024)}, u32[]{:S(2)}) copy-start(f32[4096]{0:T(1024)} %param.20) | copy-start | bytes 49156
  171.5 37.1 %all-to-all-start.3 = ((bf16[64,8,1024]{2,1,0:T(8,128)(2,1)}), bf16[64,8,1024]{2,1,0:T(8,128)(2,1)}, u32[]{:S(2)}, u32[]{:S(2)}) async-start(bf16[64,8,1024]{2,1,0:T(8,128)(2,1)} %reduce_sum.59), calls=%async_computation.3 | async-start | bytes 2097152 | tf_op jit(solution)/shard_map/all_to_all | solution.py:155
  210.1 15.1 %copy-start.5 = (bf16[32,1024]{1,0:T(8,128)(2,1)}, bf16[32,1024]{1,0:T(8,128)(2,1)S(1)}, u32[]{:S(2)}) copy-start(bf16[32,1024]{1,0:T(8,128)(2,1)S(1)} %fusion.40) | copy-start | bytes 196612
  210.9 10.1 %all-to-all-start.4 = ((bf16[4,32,1024]{2,1,0:T(8,128)(2,1)}), bf16[4,32,1024]{2,1,0:T(8,128)(2,1)S(1)}, u32[]{:S(2)}, u32[]{:S(2)}) async-start(bf16[4,32,1024]{2,1,0:T(8,128)(2,1)} %broadcast_in_dim.81), calls=%async_computation.4 | async-start | bytes 524288 | tf_op jit(solution)/shard_map/all_to_all | solution.py:30
  220.9 3.3 %copy-start.3 = (f32[1,1,16,32,128]{4,3,2,1,0:T(8,128)S(1)}, f32[1,1,16,32,128]{4,3,2,1,0:T(8,128)}, u32[]{:S(2)}) copy-start(f32[1,1,16,32,128]{4,3,2,1,0:T(8,128)} %get-tuple-element.7) | copy-start | bytes 786436
  220.9 3.6 %copy-start.2 = (bf16[4096,128]{1,0:T(8,128)(2,1)S(1)}, bf16[4096,128]{1,0:T(8,128)(2,1)}, u32[]{:S(2)}) copy-start(bf16[4096,128]{1,0:T(8,128)(2,1)} %param.22) | copy-start | bytes 3145732
  220.9 3.9 %copy-start.12 = (bf16[1,128,128]{2,1,0:T(8,128)(2,1)S(1)}, bf16[1,128,128]{2,1,0:T(8,128)(2,1)}, u32[]{:S(2)}) copy-start(bf16[1,128,128]{2,1,0:T(8,128)(2,1)} %param.25) | copy-start | bytes 98308
  222.9 3.3 %copy-start.7 = (bf16[32,128]{1,0:T(8,128)(2,1)}, bf16[32,128]{1,0:T(8,128)(2,1)S(1)}, u32[]{:S(2)}) copy-start(bf16[32,128]{1,0:T(8,128)(2,1)S(1)} %convolution_convert_fusion.3) | copy-start | bytes 24580
  224.9 1.4 copy-start.9
